TPU v7x, 256 devices: a whole 4x4x8 slice. The times are simulated.
256 devices in a mesh: sky: 32 (over z, x), exp: 8 (over y, core).
Axes of the slice: x: 4, y: 4, z: 8, core: 2. Of those that a mesh axis runs over, the one named last changes fastest.
Arguments:
- sky_start: float32 [256, 128, 128], P('sky'), may hold values from 0 to 2
- observed: bfloat16 [8, 512, 4, 128, 128], P('exp', 'sky'), may hold values from -6 to 6
- src_owner: int32 [8, 512], P('exp', 'sky'), may hold values from 0 to 31, as said below
- src_local: int32 [8, 512], P('exp', 'sky'), may hold values from 0 to 7
- res_ids: int32 [8, 512, 4], P('exp', 'sky'), may hold values from 0 to 15
- psf_ids: int32 [8, 512, 4], P('exp', 'sky'), may hold values from 0 to 15
- pixel_mask: int32 [8, 512, 4, 2, 128], P('exp', 'sky'), may hold values 0 or 1
- resample: float32 [16, 128, 128], replicated, may hold values from -0.5 to 0.5
- psf: float32 [16, 128, 128], replicated, may hold values from -0.5 to 0.5
Outputs:
- estimate: float32 [256, 128, 128], P('sky')
Inputs may be any that keep to these rules, and one draw needn't show every extreme that they name: `src_owner`: each device's 16 footprint rows name any one owner at most 2 times; in every chip set one owner is named 2 times by the rows of every device.
All inputs are finite; a program needn't handle non-finite values. No bound on the sum of `pixel_mask` on one device may be relied on, other than what follows from the above.
Results may differ from a plain program's by a relative error of at most 0.002.
Values may be sent and summed in bfloat16 or wider, within the bound.
A program may use at most 128 MiB of HBM per device.

v0:
```python
import jax
import jax.numpy as jnp
from jax import lax
from jax.sharding import PartitionSpec as P

ITERS = 2


def project(modeled, observed_blk, resamp_mats, psf_mats, weight):
    hp = lax.Precision.HIGHEST
    inner = jnp.einsum("qeij,qjk->qeik", resamp_mats, modeled, precision=hp)
    predicted = jnp.einsum("qeik,qelk->qeil", inner, psf_mats, precision=hp)
    resid = weight * (predicted - observed_blk.astype(jnp.float32))
    spread = jnp.einsum("qeil,qelk->qeik", resid, psf_mats, precision=hp)
    return jnp.einsum("qeij,qeik->qjk", resamp_mats, spread, precision=hp)


def on_device(
    sky_start, observed, src_owner, src_local, res_ids, psf_ids, pixel_mask, resample, psf
):
    sky_count = lax.axis_size("sky")
    exp_count = lax.axis_size("exp")
    req_rows = src_owner.shape[1]
    expo_count = observed.shape[2]
    block_count = sky_start.shape[0]
    side_len = sky_start.shape[1]
    capacity = max(2, 2 * req_rows // sky_count)
    owners = src_owner[0]
    local_ids = src_local[0]
    owner_hits = (owners[:, None] == jnp.arange(sky_count)[None, :]).astype(jnp.int32)
    earlier = jnp.cumsum(owner_hits, axis=0) - owner_hits
    rank_in = jnp.sum(earlier * owner_hits, axis=1)
    slots = owners * capacity + rank_in
    requests = jnp.zeros((sky_count * capacity,), jnp.int32).at[slots].set(local_ids + 1)
    asked = lax.all_to_all(
        requests.reshape(sky_count, capacity), "sky", split_axis=0, concat_axis=0, tiled=True
    ).reshape(-1)
    select = (asked[:, None] - 1 == jnp.arange(block_count)[None, :]).astype(jnp.float32)
    resamp_mats = resample[res_ids[0]]
    psf_mats = psf[psf_ids[0]]
    masks = pixel_mask[0].astype(jnp.float32)
    weight = masks[:, :, 0, :, None] * masks[:, :, 1, None, :]
    observed_blk = observed[0]
    step_size = 1.0 / (2.0 * float(exp_count * req_rows * expo_count // block_count))
    estimate = sky_start
    for iteration in range(ITERS):
        rounded = estimate.astype(jnp.bfloat16)
        everything = lax.all_gather(rounded, "sky", axis=0, tiled=True)
        modeled = everything[owners * block_count + local_ids]
        back_proj = project(
            modeled.astype(jnp.float32), observed_blk, resamp_mats, psf_mats, weight
        )
        sending = (
            jnp.zeros((sky_count * capacity, side_len, side_len), jnp.float32)
            .at[slots]
            .set(back_proj)
        )
        returned = lax.all_to_all(
            sending.reshape(sky_count, capacity, side_len, side_len),
            "sky",
            split_axis=0,
            concat_axis=0,
            tiled=True,
        )
        partial_grad = jnp.einsum(
            "sb,sij->bij",
            select,
            returned.reshape(sky_count * capacity, side_len, side_len),
            precision=lax.Precision.HIGHEST,
        )
        total = lax.psum(partial_grad, "exp")
        estimate = jnp.maximum(estimate - step_size * total, 0.0)
    return estimate


def solution(mesh):
    in_specs = (
        P("sky", None, None),
        P("exp", "sky", None, None, None),
        P("exp", "sky"),
        P("exp", "sky"),
        P("exp", "sky", None),
        P("exp", "sky", None),
        P("exp", "sky", None, None, None),
        P(),
        P(),
    )
    out_specs = P("sky", None, None)
    return jax.shard_map(
        on_device, mesh=mesh, in_specs=in_specs, out_specs=out_specs, check_vma=False
    )
```

profile of v0, /device:TPU:1, one launch (start us, length us, event | category | flops | bytes accessed | tf_op | source)
XLA Modules:
  0.0 658.8 jit_solution(12992812160836063155)
XLA Ops:
  12.7 11.9 %all-to-all-start = ((s32[32,1,2]{2,1,0:T(1,128)}), s32[32,1,2]{2,1,0:T(1,128)S(1)}, u32[]{:S(2)}, u32[]{:S(2)}) async-start(s32[32,1,2]{2,1,0:T(1,128)} %bitcast.5), calls=%async_computation | async-start | bytes 32768 | tf_op jit(solution)/shard_map/all_to_all | solution.py:35
  26.3 2.8 gather_fusion
  29.1 2.8 gather_fusion.2
  32.0 79.5 %all-gather.3.cloned.1.call-done = bf16[256,128,128]{2,1,0:T(8,128)(2,1)} async-done(((bf16[8,128,128]{2,1,0:T(8,128)(2,1)}), bf16[256,128,128]{2,1,0:T(8,128)(2,1)}) %all-gather.3.cloned.1.call-update) | async-done | bytes 8388624 | tf_op jit(solution)/shard_map/all_gather | solution.py:48
  111.5 4.0 gather_fusion.1
  115.6 4.3 fusion.10
  120.0 9.1 %fusion.27 = f32[16,4,128,128]{3,2,1,0:T(8,128)S(1)} fusion(f32[16,4,128,128]{3,2,1,0:T(8,128)S(1)} %fusion.10, f32[16,4,128,128]{3,2,1,0:T(8,128)S(1)} %bitcast.81), kind=kOutput, calls=%fused_computation.54 | convolution fusion | flops 1610612736 | bytes 12582912 | tf_op jit(solution)/shard_map/qeik,qelk->qeil/dot_general | solution.py:12
  129.0 5.9 fusion
  134.9 7.5 %convolution_bitcast_fusion.1 = f32[16,128,128]{2,1,0:T(8,128)S(1)} fusion(f32[16,4,128,128]{3,2,1,0:T(8,128)S(1)} %bitcast.87, f32[16,4,128,128]{3,2,1,0:T(8,128)S(1)} %fusion), kind=kOutput, calls=%fused_computation.20 | convolution fusion | flops 1610612736 | bytes 9437184 | tf_op jit(solution)/shard_map/qeij,qeik->qjk/dot_general | solution.py:15
  142.4 2.5 broadcast.128.clone
  144.9 3.0 scatter_fusion
  147.9 7.5 %copy.29 = f32[32,2,128,128]{3,1,2,0:T(2,128)} copy(f32[32,2,128,128]{3,2,1,0:T(8,128)} %bitcast.90) | data formatting | bytes 8388608 | tf_op jit(solution)/shard_map/reshape | solution.py:59
  155.4 5.5 all-to-all-start.1
  161.3 91.8 %all-to-all-done.1 = f32[32,2,128,128]{3,1,2,0:T(2,128)} async-done(((f32[32,2,128,128]{3,1,2,0:T(2,128)}), f32[32,2,128,128]{3,1,2,0:T(2,128)}, u32[]{:S(2)}, u32[]{:S(2)}) %all-to-all-start.1) | async-done | bytes 4194336 | tf_op jit(solution)/shard_map/all_to_all | solution.py:58
  253.1 4.6 copy.30
  257.6 2.3 fusion.18
  260.0 64.5 %all-reduce.3.cloned.1.call-done = f32[8,128,128]{2,0,1:T(8,128)} async-done(((f32[8,128,128]{2,0,1:T(8,128)}), f32[8,128,128]{2,0,1:T(8,128)}) %all-reduce.3.cloned.1.call-update) | async-done | bytes 524304 | tf_op jit(solution)/shard_map/psum | solution.py:71
  324.5 2.1 fusion.13
  326.7 103.1 %all-gather.5.cloned.1.call-done = bf16[256,128,128]{2,0,1:T(8,128)(2,1)} async-done(((bf16[8,128,128]{2,0,1:T(8,128)(2,1)}), bf16[256,128,128]{2,0,1:T(8,128)(2,1)}) %all-gather.5.cloned.1.call-update) | async-done | bytes 8388624 | tf_op jit(solution)/shard_map/all_gather | solution.py:48
  429.7 12.0 %copy.32 = bf16[256,128,128]{2,1,0:T(8,128)(2,1)} copy(bf16[256,128,128]{2,0,1:T(8,128)(2,1)} %all-gather.5.cloned.1.call-done) | data formatting | bytes 16777216 | tf_op jit(solution)/shard_map/all_gather | solution.py:48
  441.7 4.0 gather_fusion.3
  445.8 4.3 fusion.8
  450.1 9.1 %fusion.28 = f32[16,4,128,128]{3,2,1,0:T(8,128)S(1)} fusion(f32[16,4,128,128]{3,2,1,0:T(8,128)S(1)} %fusion.8, f32[16,4,128,128]{3,2,1,0:T(8,128)S(1)} %bitcast.83), kind=kOutput, calls=%fused_computation.55 | convolution fusion | flops 1610612736 | bytes 12582912 | tf_op jit(solution)/shard_map/qeik,qelk->qeil/dot_general | solution.py:12
  459.1 5.9 fusion.1
  465.0 7.4 %convolution_bitcast_fusion = f32[16,128,128]{2,1,0:T(8,128)S(1)} fusion(f32[16,4,128,128]{3,2,1,0:T(8,128)S(1)} %bitcast.88, f32[16,4,128,128]{3,2,1,0:T(8,128)S(1)} %fusion.1), kind=kOutput, calls=%fused_computation.19 | convolution fusion | flops 1610612736 | bytes 9437184 | tf_op jit(solution)/shard_map/qeij,qeik->qjk/dot_general | solution.py:15
  472.4 2.5 broadcast.128
  474.9 3.0 scatter_fusion.1
  477.8 5.5 copy.34
  483.4 95.2 %all_to_all.19 = f32[32,2,128,128]{3,1,2,0:T(2,128)S(1)} all-to-all(f32[32,2,128,128]{3,1,2,0:T(2,128)S(1)} %copy.34), channel_id=1, replica_groups=mesh['sky'=32,'exp'=8] {'sky'}, dimensions={0} | all-to-all | bytes 8388608 | tf_op jit(solution)/shard_map/all_to_all | solution.py:58
  578.6 2.4 copy.35
  581.0 2.3 fusion.16
  583.3 66.4 %all-reduce.5.cloned.1.call-done = f32[8,128,128]{2,0,1:T(8,128)} async-done(((f32[8,128,128]{2,0,1:T(8,128)}), f32[8,128,128]{2,0,1:T(8,128)}) %all-reduce.5.cloned.1.call-update) | async-done | bytes 524304 | tf_op jit(solution)/shard_map/psum | solution.py:71
  (56 shorter events, 10.8 us)
Async XLA Ops:
  6.5 19.8 %copy-start = (f32[16,128,128]{2,1,0:T(8,128)S(1)}, f32[16,128,128]{2,1,0:T(8,128)}, u32[]{:S(2)}) copy-start(f32[16,128,128]{2,1,0:T(8,128)} %param.16) | copy-start | bytes 3145732
  6.5 105.0 %all-gather.3.cloned.1.call-start = ((), (), s32[]{:S(2)}) async-start(), calls=%async_computation.3 | async-start | bytes 8650752 | tf_op jit(solution)/shard_map/all_gather | solution.py:48
  12.7 142.7 %all-to-all-start = ((s32[32,1,2]{2,1,0:T(1,128)}), s32[32,1,2]{2,1,0:T(1,128)S(1)}, u32[]{:S(2)}, u32[]{:S(2)}) async-start(s32[32,1,2]{2,1,0:T(1,128)} %bitcast.5), calls=%async_computation | async-start | bytes 32768 | tf_op jit(solution)/shard_map/all_to_all | solution.py:35
  26.3 2.8 copy-start.6
  29.1 2.8 copy-start.11
  115.6 4.4 copy-start.2
  119.9 9.1 %copy-start.7 = (bf16[1,16,4,128,128]{4,3,2,1,0:T(8,128)(2,1)S(1)}, bf16[1,16,4,128,128]{4,3,2,1,0:T(8,128)(2,1)}, u32[]{:S(2)}) copy-start(bf16[1,16,4,128,128]{4,3,2,1,0:T(8,128)(2,1)} %param.10) | copy-start | bytes 6291460
  129.0 5.9 copy-start.4
  155.4 97.7 %all-to-all-start.1 = ((f32[32,2,128,128]{3,1,2,0:T(2,128)}), f32[32,2,128,128]{3,1,2,0:T(2,128)}, u32[]{:S(2)}, u32[]{:S(2)}) async-start(f32[32,2,128,128]{3,1,2,0:T(2,128)} %copy.29), calls=%async_computation.1 | async-start | bytes 8388608 | tf_op jit(solution)/shard_map/all_to_all | solution.py:58
  160.9 163.6 %all-reduce.3.cloned.1.call-start = ((), (), s32[]{:S(2)}) async-start(), calls=%async_computation.4 | async-start | bytes 1048576 | tf_op jit(solution)/shard_map/psum | solution.py:71
  257.6 66.9 %copy-start.8 = (f32[8,128,128]{2,1,0:T(8,128)S(1)}, f32[8,128,128]{2,1,0:T(8,128)}, u32[]{:S(2)}) copy-start(f32[8,128,128]{2,1,0:T(8,128)} %param.9) | copy-start | bytes 1572868
  259.9 169.8 %all-gather.5.cloned.1.call-start = ((), (), s32[]{:S(2)}) async-start(), calls=%async_computation.5 | async-start | bytes 8650752 | tf_op jit(solution)/shard_map/all_gather | solution.py:48
  326.6 323.1 %all-reduce.5.cloned.1.call-start = ((), (), s32[]{:S(2)}) async-start(), calls=%async_computation.6 | async-start | bytes 1048576 | tf_op jit(solution)/shard_map/psum | solution.py:71
  445.8 4.3 copy-start.3
  459.1 5.9 copy-start.5
  581.0 68.7 %copy-start.9 = (f32[8,128,128]{2,1,0:T(8,128)S(1)}, f32[8,128,128]{2,1,0:T(8,128)}, u32[]{:S(2)}) copy-start(f32[8,128,128]{2,1,0:T(8,128)} %param.9) | copy-start | bytes 1572868
  581.0 68.7 %copy-start.10 = (f32[8,128,128]{2,0,1:T(8,128)S(1)}, f32[8,128,128]{2,0,1:T(8,128)}, u32[]{:S(2)}) copy-start(f32[8,128,128]{2,0,1:T(8,128)} %all-reduce.3.cloned.1.call-done) | copy-start | bytes 1572868
  581.0 71.0 %copy-start.1 = (f32[16,128,128]{2,1,0:T(8,128)S(1)}, f32[16,128,128]{2,1,0:T(8,128)}, u32[]{:S(2)}) copy-start(f32[16,128,128]{2,1,0:T(8,128)} %param.16) | copy-start | bytes 3145732
Sparse Core Ops, SparseCore 0:
  9.9 101.5 all-gather.2
  260.1 64.3 all-reduce.2
  327.3 102.4 all-gather.4
  583.4 66.2 all-reduce.4
where the time goes:
time: 663 us; the launch traced here: 659 us
  waiting for transfers between devices  405 us (61%)
  blocking collectives  95.2 us (14%)
  local copies, waits for them, and re-layouts  59.3 us (9%)
  matrix products  57.9 us (9%)
  starting transfers between devices  17.6 us (3%)
  between operations  13.6 us (2%)
  other arithmetic  9.77 us (1%)
    all_gather x2, waiting for transfers between devices, on_device(): everything = lax.all_gather(rounded, 'sky', axis=0, tiled=True)  183 us
    psum x2, waiting for transfers between devices, on_device(): total = lax.psum(partial_grad, 'exp')  131 us
    all_to_all x1, blocking collectives, on_device(): lax.all_to_all(sending.reshape(sky_count, capacity, side_len, side_len),...  95.2 us
    all_to_all x1, waiting for transfers between devices, on_device(): lax.all_to_all(sending.reshape(sky_count, capacity, side_len, side_len),...  91.8 us
    dot_general x2, matrix products, project(): predicted = jnp.einsum('qeik,qelk->qeil', inner, psf_mats, precision=hp)  18.1 us
    dot_general x2, matrix products, project(): return jnp.einsum('qeij,qeik->qjk', resamp_mats, spread, precision=hp)  14.9 us
  transfers between devices with their start and end apart: 6, of which 5 were waited for; matrix products, arithmetic and copies ran while one was open for 8% of the time, Pallas kernels for 0%

commit v1 on v0

v1 whole, which is shorter than its diff:
```python
import functools

import jax
import jax.numpy as jnp
from jax import lax
from jax.experimental import pallas as pl
from jax.experimental.pallas import tpu as pltpu
from jax.sharding import PartitionSpec as P

MESH = pl.DeviceIdType.MESH
BF = jnp.bfloat16
F32 = jnp.float32
I32 = jnp.int32
ITERS = 2
NZ, NRING = 8, 4
B = 128
H = 64
REQ = 16
EXPO = 4
STEP = 1.0 / 128.0
ORDER = (0, 1, 3, 2)
POS = {0: 0, 1: 1, 3: 2, 2: 3}


def coords():
    s = lax.axis_index("sky")
    e = lax.axis_index("exp")
    return s // NRING, s % NRING, e // 2, e % 2


def at(z, x, y, c):
    return (z * NRING + x, y * 2 + c)


class Net:
    def __init__(self, send, recv):
        self.send, self.recv, self.used, self.open = send, recv, 0, []
        self.z, self.x, self.y, self.c = coords()

    def along(self, axis, k):
        z, x, y, c = self.z, self.x, self.y, self.c
        if axis == "z":
            return at((z + k) % NZ, x, y, c)
        if axis == "x":
            return at(z, (x + k) % NRING, y, c)
        if axis == "y":
            return at(z, x, (y + k) % NRING, c)
        return at(z, x, y, 1 - c)

    def copy(self, src, dst, axis, k):
        i = self.used
        self.used += 1
        cp = pltpu.make_async_remote_copy(
            src_ref=src, dst_ref=dst, send_sem=self.send.at[i], recv_sem=self.recv.at[i],
            device_id=self.along(axis, k), device_id_type=MESH)
        cp.start()
        self.open.append(cp)
        return cp

    def barrier(self):
        bar = pltpu.get_barrier_semaphore()
        peers = [self.along("c", 1)]
        peers += [self.along(a, k) for a in ("x", "y") for k in (1, 2, 3)]
        peers += [self.along("z", k) for k in range(1, NZ)]
        for peer in peers:
            pl.semaphore_signal(bar, inc=1, device_id=peer, device_id_type=MESH)
        pl.semaphore_wait(bar, len(peers))

    def drain(self):
        for cp in self.open:
            cp.wait_send()


HALVES = (("x", "y", 0), ("y", "x", H))


def ring_at(net, axis):
    return net.x if axis == "x" else net.y


def gather(net, block, gz, full, slots, got, tabs, ids, out):
    gz[net.z] = block
    zc = {k: net.copy(gz.at[net.z], gz.at[net.z], "z", k) for k in (4, 3, 5, 2, 6, 1, 7)}
    for k in (1, 7, 2, 6, 3, 5, 4):
        zc[k].wait_recv()
    mid, cores = {}, []
    for k in (2, 1, 3):
        for h, (dense, _, lo) in enumerate(HALVES):
            here = pl.ds(net.c * 32 + ring_at(net, dense) * NZ, NZ)
            mid[h, k] = net.copy(gz.at[:, pl.ds(lo, H)], full[h].at[here], dense, k)
    for h, (dense, _, lo) in enumerate(HALVES):
        here = pl.ds(net.c * 32 + ring_at(net, dense) * NZ, NZ)
        cores.append(net.copy(gz.at[:, pl.ds(lo, H)], full[h].at[here], "c", 1))
        full[h][here] = gz[:, lo:lo + H]
    for k in (1, 3, 2):
        for h, (dense, _, lo) in enumerate(HALVES):
            mid[h, k].wait_recv()
            there = pl.ds(net.c * 32 + ((ring_at(net, dense) - k + NRING) % NRING) * NZ, NZ)
            cores.append(net.copy(full[h].at[there], full[h].at[there], "c", 1))
    for cp in cores:
        cp.wait_recv()
    last = {}
    for k in (2, 1, 3, 0):
        for h, (_, sparse, lo) in enumerate(HALVES):
            base = POS[(NRING - k) % NRING] * REQ
            mine = ring_at(net, sparse)

            def fill(r, carry, h=h, k=k, base=base, mine=mine):
                half = full[h][tabs[4 + h, base + r]]
                if k == 0:
                    got[h][mine, r] = half
                else:
                    slots[h][k, r] = half
                return carry

            lax.fori_loop(0, REQ, fill, 0, unroll=4)
            if k:
                last[h, k] = net.copy(slots[h].at[k], got[h].at[mine], sparse, k)
    for k in (1, 3, 2):
        for h in range(2):
            last[h, k].wait_recv()

    def place(r, carry):
        row = ids[r]
        out[r, 0:H] = got[0][(row // 2) % NRING, r]
        out[r, H:B] = got[1][(row // 8) % NRING, r]
        return carry

    lax.fori_loop(0, REQ, place, 0, unroll=4)


def scatter(net, back, rows, cum, core_out, core_in, ring_out, ring_own, ring_in, zout, zown, zin, tabs):
    first, cores, mids = {}, {}, {}
    for k in (2, 1, 3):
        for h, (_, sparse, lo) in enumerate(HALVES):
            first[h, k] = net.copy(back.at[:, pl.ds(lo, H)], rows[h].at[k], sparse, k)
    for k in ORDER:
        for h, (_, sparse, lo) in enumerate(HALVES):
            if k:
                first[h, k].wait_recv()

            def add(r, carry, h=h, k=k, lo=lo):
                p = POS[k] * REQ + r
                prev = tabs[2 * h, p]
                term = back[r, lo:lo + H] if k == 0 else rows[h][k, r]
                before = cum[h][jnp.maximum(prev, 0)]
                cum[h][p] = term.astype(F32) + jnp.where(prev >= 0, before, 0.0)
                return carry

            lax.fori_loop(0, REQ, add, 0, unroll=4)

    def total(h, key):
        at_last = tabs[2 * h + 1, key]
        return jnp.where(at_last >= 0, cum[h][jnp.maximum(at_last, 0)], 0.0)

    for k in (2, 1, 3, 0):
        for h, (dense, _, lo) in enumerate(HALVES):
            there = (ring_at(net, dense) + k) % NRING

            def pick(z, carry, h=h, k=k, there=there):
                core_out[h][k, z] = total(h, (1 - net.c) * 32 + there * NZ + z).astype(BF)
                return carry

            lax.fori_loop(0, NZ, pick, 0, unroll=4)
            cores[h, k] = net.copy(core_out[h].at[k], core_in[h].at[k], "c", 1)
    for k in (2, 1, 3, 0):
        for h, (dense, _, lo) in enumerate(HALVES):
            cores[h, k].wait_recv()
            there = (ring_at(net, dense) + k) % NRING

            def join(z, carry, h=h, k=k, there=there):
                both = total(h, net.c * 32 + there * NZ + z) + core_in[h][k, z].astype(F32)
                if k:
                    ring_out[h][k, z] = both.astype(BF)
                else:
                    ring_own[h][z] = both
                return carry

            lax.fori_loop(0, NZ, join, 0, unroll=4)
            if k:
                mids[h, k] = net.copy(ring_out[h].at[k], ring_in[h].at[k], dense, k)
    for h in range(2):
        for k in (1, 3, 2):
            mids[h, k].wait_recv()
    for h, (_, _, lo) in enumerate(HALVES):

        def ring(z, carry, h=h, lo=lo):
            both = ring_own[h][z]
            for k in (1, 3, 2):
                both = both + ring_in[h][k, z].astype(F32)
            zout[z, lo:lo + H] = both.astype(BF)
            zown[z, lo:lo + H] = both
            return carry

        lax.fori_loop(0, NZ, ring, 0, unroll=4)
    zc = {k: net.copy(zout.at[(net.z + k) % NZ], zin.at[k], "z", k) for k in (4, 3, 5, 2, 6, 1, 7)}
    grad = zown[net.z]
    for k in (1, 7, 2, 6, 3, 5, 4):
        zc[k].wait_recv()
        grad = grad + zin[k].astype(F32)
    return grad


def tables(net, seen, tab_ref):
    lane = lax.broadcasted_iota(I32, (B, B), 1)
    sub = lax.broadcasted_iota(I32, (B, B), 0)
    for h in range(2):
        ids = sum(seen[h, k, POS[k]:POS[k] + 1, :] for k in range(NRING))
        zz, xx, yy, cc = ids // 32, (ids // 8) % 4, (ids // 2) % 4, ids % 2
        ring = xx if h == 0 else yy
        index = cc * 32 + ring * NZ + zz
        mine = (yy == net.y) if h == 0 else (xx == net.x)
        real = lane[0:1] < NRING * REQ
        key = jnp.where(jnp.logical_and(mine, real), index, -1).astype(F32)
        column = jnp.sum(jnp.where(lane == sub, jnp.broadcast_to(key, (B, B)), 0.0), axis=1, keepdims=True)
        same = jnp.logical_and(column == key, column >= 0.0)
        earlier = jnp.logical_and(same, sub < lane)
        prev = jnp.max(jnp.where(earlier, sub.astype(F32), -1.0), axis=0, keepdims=True)
        final = jnp.max(jnp.where(column == lane.astype(F32), sub.astype(F32), -1.0), axis=0, keepdims=True)
        tab_ref[2 * h:2 * h + 1, :] = prev.astype(I32)
        tab_ref[2 * h + 1:2 * h + 2, :] = final.astype(I32)
        tab_ref[4 + h:5 + h, :] = index
    tab_ref[6:8, :] = jnp.zeros((2, B), I32)


GATHER = [
    pltpu.VMEM((NZ, B, B), BF),
    pltpu.VMEM((64, H, B), BF), pltpu.VMEM((64, H, B), BF),
    pltpu.VMEM((NRING, REQ, H, B), BF), pltpu.VMEM((NRING, REQ, H, B), BF),
    pltpu.VMEM((NRING, REQ, H, B), BF), pltpu.VMEM((NRING, REQ, H, B), BF),
]
SCATTER = [
    pltpu.VMEM((NRING, REQ, H, B), BF), pltpu.VMEM((NRING, REQ, H, B), BF),
    pltpu.VMEM((64, H, B), F32), pltpu.VMEM((64, H, B), F32),
    pltpu.VMEM((NRING, NZ, H, B), BF), pltpu.VMEM((NRING, NZ, H, B), BF),
    pltpu.VMEM((NRING, NZ, H, B), BF), pltpu.VMEM((NRING, NZ, H, B), BF),
    pltpu.VMEM((NRING, NZ, H, B), BF), pltpu.VMEM((NRING, NZ, H, B), BF),
    pltpu.VMEM((NZ, H, B), F32), pltpu.VMEM((NZ, H, B), F32),
    pltpu.VMEM((NRING, NZ, H, B), BF), pltpu.VMEM((NRING, NZ, H, B), BF),
    pltpu.VMEM((NZ, B, B), BF), pltpu.VMEM((NZ, B, B), F32), pltpu.VMEM((NZ, B, B), BF),
]


def sems(n):
    return [pltpu.SemaphoreType.DMA((n,)), pltpu.SemaphoreType.DMA((n,))]


def pair(refs, i):
    return (refs[i], refs[i + 1])


def unpack_gather(refs):
    return refs[0], pair(refs, 1), pair(refs, 3), pair(refs, 5)


def unpack_scatter(refs):
    return (pair(refs, 0), pair(refs, 2), pair(refs, 4), pair(refs, 6), pair(refs, 8),
            pair(refs, 10), pair(refs, 12), refs[14], refs[15], refs[16])


def first_kernel(sky, idtile, ids, model, tab, seen, tab_smem, local_sem, send, recv, *refs):
    gz, full, slots, got = unpack_gather(refs)
    net = Net(send, recv)
    net.barrier()
    told = []
    for h, (_, sparse, _) in enumerate(HALVES):
        seen[h, 0] = idtile[...]
        for k in (1, 2, 3):
            told.append(net.copy(idtile, seen.at[h, k], sparse, k))
    for cp in told:
        cp.wait_recv()
    tables(net, seen, tab)
    cp = pltpu.make_async_copy(tab, tab_smem, local_sem)
    cp.start()
    cp.wait()
    block = sky[net.y * 2 + net.c].astype(BF)
    gather(net, block, gz, full, slots, got, tab_smem, ids, model)
    net.drain()


def between_kernel(back, sky, tabs, ids, model, estimate, send, recv, *refs):
    gz, full, slots, got = unpack_gather(refs[:7])
    net = Net(send, recv)
    net.barrier()
    grad = scatter(net, back, *unpack_scatter(refs[7:]), tabs)
    new = jnp.maximum(sky[net.y * 2 + net.c] - STEP * grad, 0.0)
    estimate[...] = new
    gather(net, new.astype(BF), gz, full, slots, got, tabs, ids, model)
    net.drain()


def last_kernel(back, estimate, tabs, out, held, send, recv, *refs):
    net = Net(send, recv)
    net.barrier()
    grad = scatter(net, back, *unpack_scatter(refs), tabs)
    mine = net.y * 2 + net.c
    held[mine] = jnp.maximum(estimate[...] - STEP * grad, 0.0)
    ring = {k: net.copy(held.at[mine], held.at[mine], "y", k) for k in (2, 1, 3)}
    cores = [net.copy(held.at[mine], held.at[mine], "c", 1)]
    for k in (1, 3, 2):
        ring[k].wait_recv()
        there = ((net.y - k + NRING) % NRING) * 2 + net.c
        cores.append(net.copy(held.at[there], held.at[there], "c", 1))
    for cp in cores:
        cp.wait_recv()
    out[...] = held[...]
    net.drain()


VM = pl.BlockSpec(memory_space=pltpu.VMEM)
SM = pl.BlockSpec(memory_space=pltpu.SMEM)


def params(cid):
    return pltpu.CompilerParams(collective_id=cid, has_side_effects=True, vmem_limit_bytes=56 * 2**20)


ROWS_STEP = 2


def project_kernel(res, psf, model, obs, mask, rm, rt, pm, pt, out):
    step = pl.program_id(0)
    for q in range(ROWS_STEP):
        r_ids = [res[(step * ROWS_STEP + q) * EXPO + x] for x in range(EXPO)]
        p_ids = [psf[(step * ROWS_STEP + q) * EXPO + x] for x in range(EXPO)]
        rows = jnp.concatenate([rm[i] for i in r_ids], axis=0)
        inner = jnp.dot(rows, model[q], preferred_element_type=F32).astype(BF)
        spread, cols = [], []
        for x in range(EXPO):
            predicted = jnp.dot(inner[x * B:(x + 1) * B], pt[p_ids[x]], preferred_element_type=F32)
            good = mask[q, x].astype(F32)
            resid = (predicted - obs[q, x].astype(F32)) * good[1:2]
            spread.append(jnp.dot(resid.astype(BF), pm[p_ids[x]], preferred_element_type=F32).astype(BF))
            cols.append(rt[r_ids[x]] * good[0:1].astype(BF))
        out[q] = jnp.dot(jnp.concatenate(cols, axis=1), jnp.concatenate(spread, axis=0),
                         preferred_element_type=F32).astype(BF)


def project(res, psf, model, obs, mask, rm, rt, pm, pt):
    table = pl.BlockSpec((16, B, B), lambda i, *_: (0, 0, 0))
    return pl.pallas_call(
        project_kernel, name="project",
        grid_spec=pltpu.PrefetchScalarGridSpec(
            num_scalar_prefetch=2, grid=(REQ // ROWS_STEP,),
            in_specs=[
                pl.BlockSpec((ROWS_STEP, B, B), lambda i, *_: (i, 0, 0)),
                pl.BlockSpec((ROWS_STEP, EXPO, B, B), lambda i, *_: (i, 0, 0, 0)),
                pl.BlockSpec((ROWS_STEP, EXPO, 2, B), lambda i, *_: (i, 0, 0, 0)),
                table, table, table, table],
            out_specs=pl.BlockSpec((ROWS_STEP, B, B), lambda i, *_: (i, 0, 0))),
        out_shape=jax.ShapeDtypeStruct((REQ, B, B), BF),
        compiler_params=pltpu.CompilerParams(vmem_limit_bytes=32 * 2**20),
    )(res, psf, model, obs, mask, rm, rt, pm, pt)


def on_device(sky, observed, src_owner, src_local, res_ids, psf_ids, pixel_mask, resample, psf):
    ids = src_owner[0] * 8 + src_local[0]
    idtile = jnp.zeros((8, B), I32)
    for j in range(NRING):
        idtile = idtile.at[j, j * REQ:(j + 1) * REQ].set(ids)
    rm, pm = resample.astype(BF), psf.astype(BF)
    rt, pt = rm.transpose(0, 2, 1), pm.transpose(0, 2, 1)
    model_shape = jax.ShapeDtypeStruct((REQ, B, B), BF)
    model, tabs = pl.pallas_call(
        first_kernel, name="first_gather",
        out_shape=(model_shape, jax.ShapeDtypeStruct((8, B), I32)),
        in_specs=[VM, VM, SM], out_specs=(VM, VM),
        scratch_shapes=[pltpu.VMEM((2, NRING, 8, B), I32), pltpu.SMEM((8, B), I32),
                        pltpu.SemaphoreType.DMA] + sems(40) + GATHER,
        compiler_params=params(0))(sky, idtile, ids)
    fixed = (observed[0], pixel_mask[0], rm, rt, pm, pt)
    res, pids = res_ids[0].reshape(-1), psf_ids[0].reshape(-1)
    back = project(res, pids, model, *fixed)
    model, estimate = pl.pallas_call(
        between_kernel, name="reduce_gather",
        out_shape=(model_shape, jax.ShapeDtypeStruct((B, B), F32)),
        in_specs=[VM, VM, SM, SM], out_specs=(VM, VM),
        scratch_shapes=sems(64) + GATHER + SCATTER,
        compiler_params=params(1))(back, sky, tabs, ids)
    back = project(res, pids, model, *fixed)
    return pl.pallas_call(
        last_kernel, name="reduce_last",
        out_shape=jax.ShapeDtypeStruct((8, B, B), F32),
        in_specs=[VM, VM, SM], out_specs=VM,
        scratch_shapes=[pltpu.VMEM((8, B, B), F32)] + sems(40) + SCATTER,
        compiler_params=params(2))(back, estimate, tabs)


def solution(mesh):
    in_specs = (
        P("sky", None, None),
        P("exp", "sky", None, None, None),
        P("exp", "sky"),
        P("exp", "sky"),
        P("exp", "sky", None),
        P("exp", "sky", None),
        P("exp", "sky", None, None, None),
        P(),
        P(),
    )
    return jax.shard_map(
        on_device, mesh=mesh, in_specs=in_specs, out_specs=P("sky", None, None), check_vma=False
    )
```

time: 663 us -> 197 us (0.30)
  waiting for transfers between devices: 405 us -> 0 us
  Pallas kernels: 0 us -> 181 us
  blocking collectives: 95.2 us -> 0 us
  matrix products: 57.9 us -> 0 us
  local copies, waits for them, and re-layouts: 59.3 us -> 15.2 us
  starting transfers between devices: 17.6 us -> 0 us
  between operations: 13.6 us -> 0.17 us
  other arithmetic: 9.77 us -> 0.67 us
    all_gather x2 -> x0, waiting for transfers between devices: 183 us -> none  [on_device(): everything = lax.all_gather(rounded, 'sky', axis=0, tiled=True)]
    pallas_call x0 -> x5, Pallas kernels: none -> 181 us  [the longest x1 70.3 us: on_device(): pl.pallas_call(between_kernel, name='reduce_gather', out_shape=(model_sha...]
    psum x2 -> x0, waiting for transfers between devices: 131 us -> none  [on_device(): total = lax.psum(partial_grad, 'exp')]
    all_to_all x1 -> x0, blocking collectives: 95.2 us -> none  [on_device(): lax.all_to_all(sending.reshape(sky_count, capacity, side_len, side_len),...]
    all_to_all x2 -> x0, waiting for transfers between devices: 91.8 us -> none  [the longest x1 91.8 us: on_device(): lax.all_to_all(sending.reshape(sky_count, capacity, side_len, side_len),...]
    dot_general x10 -> x0, matrix products: 57.9 us -> none  [the longest x2 18.1 us: project(): predicted = jnp.einsum('qeik,qelk->qeil', inner, psf_mats, precision=hp)]
    all_to_all x2 -> x0, starting transfers between devices: 17.3 us -> none  [the longest x1 11.9 us: on_device(): lax.all_to_all(requests.reshape(sky_count, capacity), 'sky', split_axis=0...]
    gather x4 -> x0, local copies, waits for them, and re-layouts: 13.6 us -> none  [the longest x2 8.05 us: on_device(): modeled = everything[owners * block_count + local_ids]]
  transfers between devices with their start and end apart: 6 -> 0, of which waited for: 5 -> 0; matrix products, arithmetic and copies ran while one was open for 8% -> 0% of each run, Pallas kernels for 0% -> 0%
where the time goes in v1:
time: 197 us
  Pallas kernels  181 us (92%)
  local copies, waits for them, and re-layouts  15.2 us (8%)
    pallas_call x1, Pallas kernels, on_device(): pl.pallas_call(between_kernel, name='reduce_gather', out_shape=(model_sha...  70.3 us
    pallas_call x1, Pallas kernels, on_device(): pl.pallas_call(first_kernel, name='first_gather', out_shape=(model_shape,...  46.2 us
    pallas_call x1, Pallas kernels, on_device(): pl.pallas_call(last_kernel, name='reduce_last', out_shape=jax.ShapeDtypeS...  42.7 us
    pallas_call x2, Pallas kernels, project(): pl.pallas_call(project_kernel, name='project', grid_spec=pltpu.PrefetchSc...  21.3 us
    unnamed x29, local copies, waits for them, and re-layouts  12.2 us

profile of v1, /device:TPU:1, one launch (start us, length us, event | category | flops | bytes accessed | tf_op | source)
XLA Modules:
  0.0 196.6 jit_solution(15068016527371521117)
XLA Ops:
  0.0 0.7 multiply_add_fusion
  0.7 0.3 scatter.15
  1.0 0.3 scatter.16
  1.3 0.3 scatter.19.idtile
  1.5 0.8 copy.18
  2.3 0.1 reshape_squeeze.6.res
  2.4 0.8 copy.19
  3.2 0.1 reshape_squeeze.7.psf
  3.2 1.5 copy.20
  4.7 0.0 copy-start
  4.8 0.0 copy-start.9
  4.8 1.0 copy.22.rm
  5.8 1.5 copy.21
  7.3 0.0 copy-done.10
  7.3 0.0 copy-done.11
  7.3 1.0 copy.23.pm
  8.3 46.2 %first_gather.1 = (bf16[16,128,128]{2,1,0:T(8,128)(2,1)}, s32[8,128]{1,0:T(8,128)}) custom-call(f32[8,128,128]{2,1,0:T(8,128)} %sky.3, s32[8,128]{1,0:T(8,128)} %copy-done.11, s32[16]{0:T(128)} %bitcast.13), custom_call_target="tpu_custom_call" | custom-call | tf_op jit(solution)/shard_map/first_gather/pallas_call | solution.py:364
  54.6 0.0 copy-done
  54.6 0.0 copy-done.9
  54.6 0.0 copy-start.1
  54.6 1.0 copy-done.1
  55.7 1.0 copy-done.3
  56.7 1.0 copy-done.8
  57.7 10.7 %project.2.back = bf16[16,128,128]{2,1,0:T(8,128)(2,1)S(1)} custom-call(s32[64]{0:T(128)S(1)} %reshape_squeeze.6.res, s32[64]{0:T(128)S(1)} %reshape_squeeze.7.psf, bf16[16,128,128]{2,1,0:T(8,128)(2,1)S(1)} %copy-done.8, bf16[16,4,128,128]{3,2,1,0:T(8,128)(2,1)S(1)} %bitcast.9, s32[16,4,2,128]{3,2,1,0:T(2,128)S(1)} %bitcast.11, ...), custom_call_target="tpu_custom_call" | custom-call | tf_op jit(solution)/shard_map/project/pallas_call | solution.py:341
  68.4 0.8 copy-done.6
  69.2 70.3 %reduce_gather.1 = (bf16[16,128,128]{2,1,0:T(8,128)(2,1)}, f32[128,128]{1,0:T(8,128)}) custom-call(bf16[16,128,128]{2,1,0:T(8,128)(2,1)} %copy-done.6, f32[8,128,128]{2,1,0:T(8,128)} %sky.3, s32[8,128]{1,0:T(8,128)} %get-tuple-element.58.tabs, s32[16]{0:T(128)} %bitcast.14), custom_call_target="tpu_custom_call" | custom-call | tf_op jit(solution)/shard_map/reduce_gather/pallas_call | solution.py:374
  139.5 1.0 copy-done.7
  140.6 10.7 %project.3.back = bf16[16,128,128]{2,1,0:T(8,128)(2,1)S(1)} custom-call(s32[64]{0:T(128)S(1)} %reshape_squeeze.6.res, s32[64]{0:T(128)S(1)} %reshape_squeeze.7.psf, bf16[16,128,128]{2,1,0:T(8,128)(2,1)S(1)} %copy-done.7, bf16[16,4,128,128]{3,2,1,0:T(8,128)(2,1)S(1)} %bitcast.10, s32[16,4,2,128]{3,2,1,0:T(2,128)S(1)} %bitcast.12, ...), custom_call_target="tpu_custom_call" | custom-call | tf_op jit(solution)/shard_map/project/pallas_call | solution.py:341
  151.2 0.0 copy-start.5
  151.3 0.8 copy-done.5
  152.0 42.7 %reduce_last.1 = f32[8,128,128]{2,1,0:T(8,128)} custom-call(bf16[16,128,128]{2,1,0:T(8,128)(2,1)} %copy-done.5, f32[128,128]{1,0:T(8,128)} %get-tuple-element.60.estimate, s32[8,128]{1,0:T(8,128)} %get-tuple-element.58.tabs), custom_call_target="tpu_custom_call" | custom-call | tf_op jit(solution)/shard_map/reduce_last/pallas_call | solution.py:381
  194.8 1.9 copy.30
  (11 shorter events, 0.0 us)
Async XLA Ops:
  0.7 6.6 %copy-start.10 = (s32[1,16]{1,0:T(1,128)}, s32[1,16]{1,0:T(1,128)S(1)}, u32[]{:S(2)}) copy-start(s32[1,16]{1,0:T(1,128)S(1)} %multiply_add_fusion) | copy-start | bytes 196
  1.5 5.8 %copy-start.11 = (s32[8,128]{1,0:T(8,128)}, s32[8,128]{1,0:T(8,128)S(1)}, u32[]{:S(2)}) copy-start(s32[8,128]{1,0:T(8,128)S(1)} %scatter.19.idtile) | copy-start | bytes 12292
  4.7 49.8 %copy-start = (bf16[1,16,4,128,128]{4,3,2,1,0:T(8,128)(2,1)S(1)}, bf16[1,16,4,128,128]{4,3,2,1,0:T(8,128)(2,1)}, u32[]{:S(2)}) copy-start(bf16[1,16,4,128,128]{4,3,2,1,0:T(8,128)(2,1)} %param.18) | copy-start | bytes 6291460
  4.8 49.8 %copy-start.9 = (s32[1,16,4,2,128]{4,3,2,1,0:T(2,128)S(1)}, s32[1,16,4,2,128]{4,3,2,1,0:T(2,128)}, u32[]{:S(2)}) copy-start(s32[1,16,4,2,128]{4,3,2,1,0:T(2,128)} %param.23) | copy-start | bytes 196612
  54.6 1.0 copy-start.1
  55.6 1.0 copy-start.3
  56.7 1.0 copy-start.8
  57.7 81.8 %copy-start.2 = (bf16[16,128,128]{2,1,0:T(8,128)(2,1)S(1)}, bf16[16,128,128]{2,1,0:T(8,128)(2,1)}, u32[]{:S(2)}) copy-start(bf16[16,128,128]{2,1,0:T(8,128)(2,1)} %copy.22.rm) | copy-start | bytes 1572868
  57.7 81.8 %copy-start.4 = (bf16[16,128,128]{2,1,0:T(8,128)(2,1)S(1)}, bf16[16,128,128]{2,1,0:T(8,128)(2,1)}, u32[]{:S(2)}) copy-start(bf16[16,128,128]{2,1,0:T(8,128)(2,1)} %copy.23.pm) | copy-start | bytes 1572868
  68.4 0.8 copy-start.6
  139.5 1.0 copy-start.7
  151.2 0.8 copy-start.5

commit v2 on v0

v2 whole, which is shorter than its diff:
```python
import jax
import jax.numpy as jnp
from jax import lax
from jax.experimental import pallas as pl
from jax.experimental.pallas import tpu as pltpu
from jax.sharding import PartitionSpec as P

MESH = pl.DeviceIdType.MESH
BF = jnp.bfloat16
F32 = jnp.float32
I32 = jnp.int32
ITERS = 2
NZ, NRING = 8, 4
B = 128
HALF = 64
CH = 32
REQ = 16
GROUP = 8
EXPO = 4
STEP = 1.0 / 128.0
ORDER = (0, 1, 3, 2)
POS = {0: 0, 1: 1, 3: 2, 2: 3}
FAR = (2, 1, 3)
NEAR = (1, 3, 2)
ZFAR = (4, 3, 5, 2, 6, 1, 7)
ZNEAR = (1, 7, 2, 6, 3, 5, 4)
HALVES = (("x", "y", 0), ("y", "x", HALF))
SEMS = 160


def at(z, x, y, c):
    return (z * NRING + x, y * 2 + c)


class Net:
    def __init__(self, send, recv):
        self.send, self.recv, self.used, self.open = send, recv, 0, []
        s, e = lax.axis_index("sky"), lax.axis_index("exp")
        self.z, self.x, self.y, self.c = s // NRING, s % NRING, e // 2, e % 2
        self.own = e

    def along(self, axis, k):
        z, x, y, c = self.z, self.x, self.y, self.c
        if axis == "z":
            return at((z + k) % NZ, x, y, c)
        if axis == "x":
            return at(z, (x + k) % NRING, y, c)
        if axis == "y":
            return at(z, x, (y + k) % NRING, c)
        return at(z, x, y, 1 - c)

    def on(self, axis):
        return self.x if axis == "x" else self.y

    def copy(self, src, dst, axis, k):
        i = self.used
        self.used += 1
        cp = pltpu.make_async_remote_copy(
            src_ref=src, dst_ref=dst, send_sem=self.send.at[i], recv_sem=self.recv.at[i],
            device_id=self.along(axis, k), device_id_type=MESH)
        cp.start()
        self.open.append(cp)
        return cp

    def barrier(self):
        bar = pltpu.get_barrier_semaphore()
        peers = [self.along("c", 1)]
        peers += [self.along(a, k) for a in ("x", "y") for k in (1, 2, 3)]
        peers += [self.along("z", k) for k in range(1, NZ)]
        for peer in peers:
            pl.semaphore_signal(bar, inc=1, device_id=peer, device_id_type=MESH)
        pl.semaphore_wait(bar, len(peers))


def tables(net, seen, tab):
    lane = lax.broadcasted_iota(I32, (B, B), 1)
    sub = lax.broadcasted_iota(I32, (B, B), 0)
    for h in range(2):
        ids = sum(seen[h, k, POS[k]:POS[k] + 1, :] for k in range(NRING))
        zz, xx, yy, cc = ids // 32, (ids // 8) % 4, (ids // 2) % 4, ids % 2
        ring = xx if h == 0 else yy
        index = cc * 32 + ring * NZ + zz
        mine = (yy == net.y) if h == 0 else (xx == net.x)
        real = lane[0:1] < NRING * REQ
        key = jnp.broadcast_to(jnp.where(jnp.logical_and(mine, real), index, -1), (B, B))
        other = key.T
        earlier = jnp.logical_and(jnp.logical_and(key == other, key >= 0), sub < lane)
        tab[2 * h:2 * h + 1, :] = jnp.max(jnp.where(earlier, sub, -1), axis=0, keepdims=True)
        tab[2 * h + 1:2 * h + 2, :] = jnp.max(jnp.where(other == lane, sub, -1), axis=0, keepdims=True)
        tab[4 + h:5 + h, :] = index
    tab[6:8, :] = jnp.zeros((2, B), I32)


def wait_sends(copies):
    for cp in copies:
        cp.wait_send()


def id_tile(ids):
    lane = lax.broadcasted_iota(I32, (8, B), 1)
    sub = lax.broadcasted_iota(I32, (8, B), 0)
    tile = jnp.zeros((8, B), I32)
    for r, block in enumerate(ids):
        spot = (r // GROUP) * NRING * GROUP + sub * GROUP + r % GROUP
        tile = jnp.where(jnp.logical_and(lane == spot, sub < NRING), block, tile)
    return tile


def place(group, k, r):
    return group * NRING * GROUP + POS[k] * GROUP + r


def send_block(net, est, gz, q):
    gz[q, net.z] = est[q].astype(BF)
    return {k: net.copy(gz.at[q, net.z], gz.at[q, net.z], "z", k) for k in ZFAR}


def gather(net, zc, gz, full, slots, got, tabs):
    mid, cores, last = {}, {0: [], 1: []}, {0: [], 1: []}
    for q in range(2):
        for k in ZNEAR:
            zc[q][k].wait_recv()
        for k in FAR:
            for h, (dense, _, _) in enumerate(HALVES):
                here = pl.ds(net.c * 32 + net.on(dense) * NZ, NZ)
                mid[q, h, k] = net.copy(gz.at[q, :, pl.ds(h * CH, CH)], full[h][q].at[here], dense, k)
        for h, (dense, _, _) in enumerate(HALVES):
            here = pl.ds(net.c * 32 + net.on(dense) * NZ, NZ)
            cores[q].append(net.copy(gz.at[q, :, pl.ds(h * CH, CH)], full[h][q].at[here], "c", 1))
            full[h][q][here] = gz[q, :, h * CH:(h + 1) * CH]

    def slot(group, q):
        for k in FAR + (0,):
            back_k = (NRING - k) % NRING

            def fill(r, carry):
                for h, (_, sparse, _) in enumerate(HALVES):
                    piece = full[h][q][jnp.clip(tabs[4 + h, place(group, back_k, r)], 0, 63)]
                    if k == 0:
                        got[h][group][net.on(sparse), q, r] = piece
                    else:
                        slots[h][k, q, group * GROUP + r] = piece
                return carry

            lax.fori_loop(0, GROUP, fill, 0, unroll=GROUP)
            if k:
                part = pl.ds(group * GROUP, GROUP)
                for h, (_, sparse, _) in enumerate(HALVES):
                    last[group].append(net.copy(
                        slots[h].at[k, q, part], got[h][group].at[net.on(sparse), q], sparse, k))

    for q in range(2):
        for k in NEAR:
            for h, (dense, _, _) in enumerate(HALVES):
                mid[q, h, k].wait_recv()
                there = pl.ds(net.c * 32 + ((net.on(dense) - k + NRING) % NRING) * NZ, NZ)
                cores[q].append(net.copy(full[h][q].at[there], full[h][q].at[there], "c", 1))
        for cp in cores[q]:
            cp.wait_recv()
        slot(0, q)
    for q in range(2):
        slot(1, q)
    return last


def products(group, got, back, owner, inner_id, res, psf, obs, mask, rm, rt, pm, pt):
    def row(i):
        r = group * GROUP + i
        ysrc, xsrc = (inner_id[0, r] // 2) % NRING, owner[0, r] % NRING
        model = jnp.concatenate(
            [got[0][group][ysrc, 0, i], got[0][group][ysrc, 1, i],
             got[1][group][xsrc, 0, i], got[1][group][xsrc, 1, i]], axis=0)
        r_ids = [res[x, r] for x in range(EXPO)]
        p_ids = [psf[x, r] for x in range(EXPO)]
        rows = jnp.concatenate([rm[i] for i in r_ids], axis=0)
        inner = jnp.dot(rows, model, preferred_element_type=F32).astype(BF)
        spread, cols = [], []
        for x in range(EXPO):
            predicted = jnp.dot(inner[x * B:(x + 1) * B], pt[p_ids[x]], preferred_element_type=F32)
            good = mask[r, x].astype(F32)
            resid = (predicted - obs[r, x].astype(F32)) * good[1:2]
            spread.append(jnp.dot(resid.astype(BF), pm[p_ids[x]], preferred_element_type=F32).astype(BF))
            cols.append(rt[r_ids[x]] * good[0:1].astype(BF))
        back[r] = jnp.dot(jnp.concatenate(cols, axis=1), jnp.concatenate(spread, axis=0),
                          preferred_element_type=F32).astype(BF)

    def two(i, carry):
        row(2 * i)
        row(2 * i + 1)
        return carry

    lax.fori_loop(0, GROUP // 2, two, 0)


def send_rows(net, group, back, rows):
    part, copies = pl.ds(group * GROUP, GROUP), {}
    for q in range(2) if group else range(1):
        for k in FAR:
            for h, (_, sparse, lo) in enumerate(HALVES):
                if group:
                    copies[q, h, k] = net.copy(back.at[part, pl.ds(lo + q * CH, CH)],
                                               rows[h].at[k, part, pl.ds(q * CH, CH)], sparse, k)
                else:
                    copies[q, h, k] = net.copy(back.at[part, pl.ds(lo, HALF)], rows[h].at[k, part], sparse, k)
    return copies


def scatter(net, copies, back, rows, cum, core_out, core_in, ring_out, ring_own, ring_in,
            zout, zown, zin, est, tabs, done):
    def accumulate(group, chunks):
        for k in ORDER:
            if k:
                for q in chunks if group else range(1):
                    for h in range(2):
                        copies[group][q, h, k].wait_recv()

            def add(i, carry):
                p, r = place(group, k, i), group * GROUP + i
                for h, (_, _, lo) in enumerate(HALVES):
                    prev = tabs[2 * h, p]
                    for q in chunks:
                        if k == 0:
                            term = back[r, lo + q * CH:lo + (q + 1) * CH]
                        else:
                            term = rows[h][k, r, q * CH:(q + 1) * CH]
                        before = cum[h][q, jnp.clip(prev, 0, 63)]
                        cum[h][q, p] = term.astype(F32) + jnp.where(prev >= 0, before, 0.0)
                return carry

            lax.fori_loop(0, GROUP, add, 0, unroll=GROUP)

    def total(h, q, key):
        final = tabs[2 * h + 1, key]
        return jnp.where(final >= 0, cum[h][q, jnp.clip(final, 0, 63)], 0.0)

    cores, mids = {}, {}

    def to_core(q):
        for k in FAR + (0,):

            def pick(z, carry):
                for h, (dense, _, _) in enumerate(HALVES):
                    there = (net.on(dense) + k) % NRING
                    core_out[h][q, k, z] = total(h, q, (1 - net.c) * 32 + there * NZ + z).astype(BF)
                return carry

            lax.fori_loop(0, NZ, pick, 0, unroll=NZ)
            for h in range(2):
                cores[q, h, k] = net.copy(core_out[h].at[q, k], core_in[h].at[q, k], "c", 1)

    def to_ring(q):
        for k in FAR + (0,):
            for h in range(2):
                cores[q, h, k].wait_recv()

            def join(z, carry):
                for h, (dense, _, _) in enumerate(HALVES):
                    there = (net.on(dense) + k) % NRING
                    both = total(h, q, net.c * 32 + there * NZ + z) + core_in[h][q, k, z].astype(F32)
                    if k:
                        ring_out[h][q, k, z] = both.astype(BF)
                    else:
                        ring_own[h][q, z] = both
                return carry

            lax.fori_loop(0, NZ, join, 0, unroll=NZ)
            if k:
                for h, (dense, _, _) in enumerate(HALVES):
                    mids[q, h, k] = net.copy(ring_out[h].at[q, k], ring_in[h].at[q, k], dense, k)

    accumulate(0, (0, 1))
    for q in range(2):
        accumulate(1, (q,))
        to_core(q)
        to_ring(q)
    zc = {}
    for q in range(2):
        for k in NEAR:
            for h in range(2):
                mids[q, h, k].wait_recv()

        def ring(z, carry):
            for h in range(2):
                both = ring_own[h][q, z]
                for k in NEAR:
                    both = both + ring_in[h][q, k, z].astype(F32)
                zout[q, z, h * CH:(h + 1) * CH] = both.astype(BF)
                zown[q, z, h * CH:(h + 1) * CH] = both
            return carry

        lax.fori_loop(0, NZ, ring, 0, unroll=NZ)
        zc[q] = {k: net.copy(zout.at[q, (net.z + k) % NZ], zin.at[q, k], "z", k) for k in ZFAR}
    for q in range(2):
        grad = zown[q, net.z]
        for k in ZNEAR:
            zc[q][k].wait_recv()
            grad = grad + zin[q, k].astype(F32)
        est[q] = jnp.maximum(est[q] - STEP * grad, 0.0)
        done(q)


def kernel(owner, inner_id, res, psf, mask, sky, observed, resample, psf_mats, out,
           idtile, seen, tab, tabs, r32, p32, rm, rt, pm, pt, obs, est, held, local, send, recv,
           gz, full_a0, full_a1, full_b0, full_b1, slots_a, slots_b, got_a0, got_a1, got_b0, got_b1, back, rows_a, rows_b, cum_a, cum_b,
           co_a, co_b, ci_a, ci_b, ro_a, ro_b, rw_a, rw_b, ri_a, ri_b, zout, zown, zin):
    full, got = ((full_a0, full_a1), (full_b0, full_b1)), ((got_a0, got_a1), (got_b0, got_b1))
    slots, rows = (slots_a, slots_b), (rows_a, rows_b)
    cum, core_out, core_in = (cum_a, cum_b), (co_a, co_b), (ci_a, ci_b)
    ring_out, ring_own, ring_in = (ro_a, ro_b), (rw_a, rw_b), (ri_a, ri_b)
    net = Net(send, recv)

    def fetch(src, dst, i):
        cp = pltpu.make_async_copy(src, dst, local.at[i])
        cp.start()
        return cp

    starts = [fetch(sky.at[net.own, pl.ds(h * HALF + q * CH, CH)], est.at[q, pl.ds(h * CH, CH)], 2 * h + q)
              for q in range(2) for h in range(2)]
    mats = [fetch(resample, r32, 4), fetch(psf_mats, p32, 5)]
    blocks = fetch(observed, obs, 6)
    own_ids = [owner[0, r] * 8 + inner_id[0, r] for r in range(REQ)]
    idtile[...] = id_tile(own_ids)
    net.barrier()
    told = []
    for h, (_, sparse, _) in enumerate(HALVES):
        for k in (1, 2, 3):
            told.append(net.copy(idtile, seen.at[h, k], sparse, k))
        seen[h, 0] = idtile[...]
    for cp in starts:
        cp.wait()
    zc = {q: send_block(net, est, gz, q) for q in range(2)}
    for cp in told:
        cp.wait_recv()
    tables(net, seen, tab)
    to_scalar = fetch(tab, tabs, 7)
    for cp in mats:
        cp.wait()

    def cast(i, carry):
        rm[i] = r32[i].astype(BF)
        rt[i] = r32[i].T.astype(BF)
        pm[i] = p32[i].astype(BF)
        pt[i] = p32[i].T.astype(BF)
        return carry

    lax.fori_loop(0, 16, cast, 0, unroll=2)
    to_scalar.wait()
    first = net.used
    for iteration in range(ITERS):
        last = gather(net, zc, gz, full, slots, got, tabs)
        if iteration == 0:
            blocks.wait()
        gathering, net.open = net.open, []
        copies = {}
        for group in range(2):
            for cp in last[group]:
                cp.wait_recv()
            products(group, got, back, owner, inner_id, res, psf, obs, mask, rm, rt, pm, pt)
            if group:
                wait_sends(gathering)
            copies[group] = send_rows(net, group, back, rows)
        zc, ring, cores = {}, [], []

        def done(q):
            if iteration < ITERS - 1:
                zc[q] = send_block(net, est, gz, q)
                return
            held[q, net.own] = est[q]
            cores.append(net.copy(held.at[q, net.own], held.at[q, net.own], "c", 1))
            for k in FAR:
                ring.append((q, k, net.copy(held.at[q, net.own], held.at[q, net.own], "y", k)))

        scatter(net, copies, back, rows, cum, core_out, core_in, ring_out, ring_own, ring_in,
                zout, zown, zin, est, tabs, done)
        if iteration < ITERS - 1:
            ahead = [cp for q in range(2) for cp in zc[q].values()]
            wait_sends([cp for cp in net.open if not any(cp is other for other in ahead)])
            net.open = ahead
            net.used = first
    for q, k, cp in ring:
        cp.wait_recv()
        there = ((net.y - k + NRING) % NRING) * 2 + net.c
        cores.append(net.copy(held.at[q, there], held.at[q, there], "c", 1))
    for cp in cores:
        cp.wait_recv()
    for q in range(2):
        for h in range(2):
            out[:, h * HALF + q * CH:h * HALF + (q + 1) * CH] = held[q, :, h * CH:(h + 1) * CH]
    wait_sends(net.open)


def twice(*shape_dtype):
    return [pltpu.VMEM(*shape_dtype)] * 2


SCRATCH = (
    [pltpu.VMEM((8, B), I32), pltpu.VMEM((2, NRING, 8, B), I32), pltpu.VMEM((8, B), I32), pltpu.SMEM((8, B), I32)]
    + twice((16, B, B), F32) + twice((16, B, B), BF) + twice((16, B, B), BF)
    + [pltpu.VMEM((REQ, EXPO, B, B), BF), pltpu.VMEM((2, HALF, B), F32), pltpu.VMEM((2, 8, HALF, B), F32)]
    + [pltpu.SemaphoreType.DMA((8,)), pltpu.SemaphoreType.DMA((SEMS,)), pltpu.SemaphoreType.DMA((SEMS,))]
    + [pltpu.VMEM((2, NZ, HALF, B), BF)]
    + twice((64, CH, B), BF) + twice((64, CH, B), BF) + twice((NRING, 2, REQ, CH, B), BF)
    + twice((NRING, 2, GROUP, CH, B), BF) + twice((NRING, 2, GROUP, CH, B), BF)
    + [pltpu.VMEM((REQ, B, B), BF)]
    + twice((NRING, REQ, HALF, B), BF) + twice((2, 64, CH, B), F32)
    + twice((2, NRING, NZ, CH, B), BF) + twice((2, NRING, NZ, CH, B), BF)
    + twice((2, NRING, NZ, CH, B), BF) + twice((2, NZ, CH, B), F32) + twice((2, NRING, NZ, CH, B), BF)
    + [pltpu.VMEM((2, NZ, HALF, B), BF), pltpu.VMEM((2, NZ, HALF, B), F32), pltpu.VMEM((2, NZ, HALF, B), BF)]
)


def on_device(sky, observed, src_owner, src_local, res_ids, psf_ids, pixel_mask, resample, psf):
    vm = pl.BlockSpec(memory_space=pltpu.VMEM)
    sm = pl.BlockSpec(memory_space=pltpu.SMEM)
    hbm = pl.BlockSpec(memory_space=pl.ANY)
    return pl.pallas_call(
        kernel, name="landweber",
        out_shape=jax.ShapeDtypeStruct((8, B, B), F32),
        in_specs=[sm, sm, sm, sm, vm, hbm, hbm, hbm, hbm], out_specs=vm,
        scratch_shapes=SCRATCH,
        compiler_params=pltpu.CompilerParams(
            collective_id=0, has_side_effects=True, vmem_limit_bytes=60 * 2**20),
    )(src_owner, src_local, jnp.swapaxes(res_ids, 1, 2)[0], jnp.swapaxes(psf_ids, 1, 2)[0], pixel_mask[0],
      sky, observed[0], resample, psf)


def solution(mesh):
    in_specs = (
        P("sky", None, None),
        P("exp", "sky", None, None, None),
        P("exp", "sky"),
        P("exp", "sky"),
        P("exp", "sky", None),
        P("exp", "sky", None),
        P("exp", "sky", None, None, None),
        P(),
        P(),
    )
    return jax.shard_map(
        on_device, mesh=mesh, in_specs=in_specs, out_specs=P("sky", None, None), check_vma=False
    )
```

time: 663 us -> 126 us (0.19)
  waiting for transfers between devices: 405 us -> 0 us
  Pallas kernels: 0 us -> 123 us
  blocking collectives: 95.2 us -> 0 us
  matrix products: 57.9 us -> 0 us
  local copies, waits for them, and re-layouts: 59.3 us -> 1.87 us
  starting transfers between devices: 17.6 us -> 0 us
  between operations: 13.6 us -> 0.01 us
  other arithmetic: 9.77 us -> 0 us
    all_gather x2 -> x0, waiting for transfers between devices: 183 us -> none  [on_device(): everything = lax.all_gather(rounded, 'sky', axis=0, tiled=True)]
    psum x2 -> x0, waiting for transfers between devices: 131 us -> none  [on_device(): total = lax.psum(partial_grad, 'exp')]
    pallas_call x0 -> x1, Pallas kernels: none -> 123 us  [on_device(): pl.pallas_call(kernel, name='landweber', out_shape=jax.ShapeDtypeStruct((...]
    all_to_all x1 -> x0, blocking collectives: 95.2 us -> none  [on_device(): lax.all_to_all(sending.reshape(sky_count, capacity, side_len, side_len),...]
    all_to_all x2 -> x0, waiting for transfers between devices: 91.8 us -> none  [the longest x1 91.8 us: on_device(): lax.all_to_all(sending.reshape(sky_count, capacity, side_len, side_len),...]
    dot_general x10 -> x0, matrix products: 57.9 us -> none  [the longest x2 18.1 us: project(): predicted = jnp.einsum('qeik,qelk->qeil', inner, psf_mats, precision=hp)]
    all_to_all x2 -> x0, starting transfers between devices: 17.3 us -> none  [the longest x1 11.9 us: on_device(): lax.all_to_all(requests.reshape(sky_count, capacity), 'sky', split_axis=0...]
    gather x4 -> x0, local copies, waits for them, and re-layouts: 13.6 us -> none  [the longest x2 8.05 us: on_device(): modeled = everything[owners * block_count + local_ids]]
  transfers between devices with their start and end apart: 6 -> 0, of which waited for: 5 -> 0; matrix products, arithmetic and copies ran while one was open for 8% -> 0% of each run, Pallas kernels for 0% -> 0%
where the time goes in v2:
time: 126 us; the launch traced here: 125 us
  Pallas kernels  123 us (98%)
  local copies, waits for them, and re-layouts  1.87 us (1%)
    pallas_call x1, Pallas kernels, on_device(): pl.pallas_call(kernel, name='landweber', out_shape=jax.ShapeDtypeStruct((...  123 us

profile of v2, /device:TPU:1, one launch (start us, length us, event | category | flops | bytes accessed | tf_op | source)
XLA Modules:
  0.0 125.4 jit_solution(15073420040526944205)
XLA Ops:
  0.0 123.5 %landweber.1 = f32[8,128,128]{2,1,0:T(8,128)} custom-call(s32[1,16]{1,0:T(1,128)} %owner.1, s32[1,16]{1,0:T(1,128)} %inner_id.1, s32[4,16]{1,0:T(4,128)} %bitcast.10, s32[4,16]{1,0:T(4,128)} %bitcast.11, s32[16,4,2,128]{3,2,1,0:T(2,128)} %bitcast.9, f32[8,128,128]{2,1,0:T(8,128)} %sky.1, bf16[16,4,128,128]{3,2,1,0:T(8,128)(2,1)} %bitcast.8, ...), custom_call_target="tpu_custom_call" | custom-call | tf_op jit(solution)/shard_map/landweber/pallas_call | solution.py:416
  123.5 1.9 %copy.11 = f32[8,128,128]{2,1,0:T(8,128)} copy(f32[8,128,128]{2,1,0:T(8,128)} %landweber.1) | data formatting | bytes 1048576

commit v3 on v2

v3 whole, which is shorter than its diff:
```python
import jax
import jax.numpy as jnp
from jax import lax
from jax.experimental import pallas as pl
from jax.experimental.pallas import tpu as pltpu
from jax.sharding import PartitionSpec as P

MESH = pl.DeviceIdType.MESH
BF = jnp.bfloat16
F32 = jnp.float32
I32 = jnp.int32
ITERS = 2
NZ, NRING = 8, 4
B = 128
HALF = 64
NQ = 4
CH = HALF // NQ
REQ = 16
GROUP = 8
EXPO = 4
STEP = 1.0 / 128.0
ORDER = (0, 1, 3, 2)
POS = {0: 0, 1: 1, 3: 2, 2: 3}
FAR = (1, 3, 2)
NEAR = (1, 3, 2)
ZFAR = (4, 3, 5, 2, 6, 1, 7)
ZNEAR = (1, 7, 2, 6, 3, 5, 4)
HALVES = (("x", "y", 0), ("y", "x", HALF))
SEMS = 128


def at(z, x, y, c):
    return (z * NRING + x, y * 2 + c)


class Channel:
    def __init__(self, net, whole):
        self.net, self.whole, self.i = net, whole, net.used
        net.used += 1
        net.open.append(self)

    def _copy(self, src, dst, peer):
        return pltpu.make_async_remote_copy(
            src_ref=src, dst_ref=dst, send_sem=self.net.send.at[self.i], recv_sem=self.net.recv.at[self.i],
            device_id=peer, device_id_type=MESH)

    def copy(self, src, dst, axis, k):
        self._copy(src, dst, self.net.peers[axis, k]).start()

    def wait_recv(self):
        self._copy(self.whole, self.whole, self.net.peers["c", 1]).wait_recv()

    def wait_send(self):
        self._copy(self.whole, self.whole, self.net.peers["c", 1]).wait_send()


class Net:
    def __init__(self, send, recv):
        self.send, self.recv, self.used, self.open = send, recv, 0, []
        s, e = lax.axis_index("sky"), lax.axis_index("exp")
        self.z, self.x, self.y, self.c = z, x, y, c = s // NRING, s % NRING, e // 2, e % 2
        self.own = e
        self.peers = {("c", 1): at(z, x, y, 1 - c)}
        for k in FAR:
            self.peers["x", k] = at(z, (x + k) % NRING, y, c)
            self.peers["y", k] = at(z, x, (y + k) % NRING, c)
        for k in ZFAR:
            self.peers["z", k] = at((z + k) % NZ, x, y, c)

    def on(self, axis):
        return self.x if axis == "x" else self.y

    def barrier(self):
        bar = pltpu.get_barrier_semaphore()
        for peer in self.peers.values():
            pl.semaphore_signal(bar, inc=1, device_id=peer, device_id_type=MESH)
        pl.semaphore_wait(bar, len(self.peers))


def wait_sends(channels):
    for channel in channels:
        channel.wait_send()


def tables(net, seen, tab):
    lane = lax.broadcasted_iota(I32, (B, B), 1)
    sub = lax.broadcasted_iota(I32, (B, B), 0)
    for h in range(2):
        ids = sum(seen[h, k, POS[k]:POS[k] + 1, :] for k in range(NRING))
        zz, xx, yy, cc = ids // 32, (ids // 8) % 4, (ids // 2) % 4, ids % 2
        ring = xx if h == 0 else yy
        index = cc * 32 + ring * NZ + zz
        mine = (yy == net.y) if h == 0 else (xx == net.x)
        real = lane[0:1] < NRING * REQ
        key = jnp.broadcast_to(jnp.where(jnp.logical_and(mine, real), index, -1), (B, B))
        other = key.T
        earlier = jnp.logical_and(jnp.logical_and(key == other, key >= 0), sub < lane)
        tab[2 * h:2 * h + 1, :] = jnp.max(jnp.where(earlier, sub, -1), axis=0, keepdims=True)
        tab[2 * h + 1:2 * h + 2, :] = jnp.max(jnp.where(other == lane, sub, -1), axis=0, keepdims=True)
        tab[4 + h:5 + h, :] = index
    tab[6:8, :] = jnp.zeros((2, B), I32)


def id_tile(ids):
    lane = lax.broadcasted_iota(I32, (8, B), 1)
    sub = lax.broadcasted_iota(I32, (8, B), 0)
    tile = jnp.zeros((8, B), I32)
    for r, block in enumerate(ids):
        spot = (r // GROUP) * NRING * GROUP + sub * GROUP + r % GROUP
        tile = jnp.where(jnp.logical_and(lane == spot, sub < NRING), block, tile)
    return tile


def place(group, k, r):
    return group * NRING * GROUP + POS[k] * GROUP + r


def send_block(net, est, gz, q):
    gz[q, net.z] = est[q].astype(BF)
    channel = Channel(net, gz.at[q, pl.ds(0, NZ - 1)])
    for k in ZFAR:
        channel.copy(gz.at[q, net.z], gz.at[q, net.z], "z", k)
    return channel


def gather(net, zc, gz, full, slots, got, tabs):
    mid, cores, last = {}, {}, {}
    for q in range(NQ):
        zc[q].wait_recv()
        for h in range(2):
            mid[q, h] = Channel(net, full[h][q].at[pl.ds(0, 3 * NZ)])
        for k in FAR:
            for h, (dense, _, _) in enumerate(HALVES):
                here = pl.ds(net.c * 32 + net.on(dense) * NZ, NZ)
                mid[q, h].copy(gz.at[q, :, pl.ds(h * CH, CH)], full[h][q].at[here], dense, k)
        for h, (dense, _, _) in enumerate(HALVES):
            here = pl.ds(net.c * 32 + net.on(dense) * NZ, NZ)
            full[h][q][here] = gz[q, :, h * CH:(h + 1) * CH]

    def slot(group, chunks, send):
        for k in FAR + (0,):
            back_k = (NRING - k) % NRING

            def fill(r, carry):
                for h, (_, sparse, _) in enumerate(HALVES):
                    block = jnp.clip(tabs[4 + h, place(group, back_k, r)], 0, 63)
                    for q in chunks:
                        if k == 0:
                            got[h][group][net.on(sparse), q, r] = full[h][q][block]
                        else:
                            slots[h][k, q, group * GROUP + r] = full[h][q][block]
                return carry

            lax.fori_loop(0, GROUP, fill, 0, unroll=GROUP)
            if k:
                part, qs = pl.ds(group * GROUP, GROUP), pl.ds(chunks[0], len(chunks))
                for h, (_, sparse, _) in enumerate(HALVES):
                    send[h].copy(slots[h].at[k, qs, part], got[h][group].at[net.on(sparse), qs], sparse, k)

    for q in range(NQ):
        for h in range(2):
            mid[q, h].wait_recv()
            mine = pl.ds(net.c * 32, 32)
            cores[q, h] = Channel(net, full[h][q].at[pl.ds(0, 32)])
            cores[q, h].copy(full[h][q].at[mine], full[h][q].at[mine], "c", 1)
        if q == 0:
            last[0] = [Channel(net, got[h][0].at[pl.ds(0, 3)]) for h in range(2)]
        for h in range(2):
            cores[q, h].wait_recv()
        slot(0, (q,), last[0])
    last[1] = [Channel(net, got[h][1].at[pl.ds(0, 3)]) for h in range(2)]
    slot(1, tuple(range(NQ)), last[1])
    return last


def products(group, got, back, owner, inner_id, res, psf, obs, mask, rm, rt, pm, pt):
    def row(i):
        r = group * GROUP + i
        ysrc, xsrc = (inner_id[0, r] // 2) % NRING, owner[0, r] % NRING
        model = jnp.concatenate(
            [got[0][group][ysrc, q, i] for q in range(NQ)] + [got[1][group][xsrc, q, i] for q in range(NQ)], axis=0)
        r_ids = [res[x, r] for x in range(EXPO)]
        p_ids = [psf[x, r] for x in range(EXPO)]
        rows = jnp.concatenate([rm[i] for i in r_ids], axis=0)
        inner = jnp.dot(rows, model, preferred_element_type=F32).astype(BF)
        spread, cols = [], []
        for x in range(EXPO):
            predicted = jnp.dot(inner[x * B:(x + 1) * B], pt[p_ids[x]], preferred_element_type=F32)
            good = mask[r, x].astype(F32)
            resid = (predicted - obs[r, x].astype(F32)) * good[1:2]
            spread.append(jnp.dot(resid.astype(BF), pm[p_ids[x]], preferred_element_type=F32).astype(BF))
            cols.append(rt[r_ids[x]] * good[0:1].astype(BF))
        back[r] = jnp.dot(jnp.concatenate(cols, axis=1), jnp.concatenate(spread, axis=0),
                          preferred_element_type=F32).astype(BF)

    def two(i, carry):
        for j in range(4):
            row(4 * i + j)
        return carry

    lax.fori_loop(0, GROUP // 4, two, 0)


def send_rows(net, group, back, rows):
    part, copies = pl.ds(group * GROUP, GROUP), {}
    for q in range(NQ) if group else range(1):
        size, skip = (CH, q * CH) if group else (HALF, 0)
        for h in range(2):
            copies[q, h] = Channel(net, rows[h].at[pl.ds(0, 3), part, pl.ds(skip, size)])
        for k in FAR:
            for h, (_, sparse, lo) in enumerate(HALVES):
                copies[q, h].copy(back.at[part, pl.ds(lo + skip, size)],
                                  rows[h].at[k, part, pl.ds(skip, size)], sparse, k)
    return copies


def scatter(net, copies, back, rows, cum, core_out, core_in, ring_out, ring_own, ring_in,
            zout, zown, zin, est, tabs, done):
    def accumulate(group, chunks):
        for k in ORDER:
            if k == ORDER[1]:
                for q in chunks if group else range(1):
                    for h in range(2):
                        copies[group][q, h].wait_recv()

            def add(i, carry):
                p, r = place(group, k, i), group * GROUP + i
                for h, (_, _, lo) in enumerate(HALVES):
                    prev = tabs[2 * h, p]
                    for q in chunks:
                        if k == 0:
                            term = back[r, lo + q * CH:lo + (q + 1) * CH]
                        else:
                            term = rows[h][k, r, q * CH:(q + 1) * CH]
                        before = cum[h][q, jnp.clip(prev, 0, 63)]
                        cum[h][q, p] = term.astype(F32) + jnp.where(prev >= 0, before, 0.0)
                return carry

            lax.fori_loop(0, GROUP, add, 0, unroll=GROUP)

    def total(h, q, key):
        final = tabs[2 * h + 1, key]
        return jnp.where(final >= 0, cum[h][q, jnp.clip(final, 0, 63)], 0.0)

    cores, mids = {}, {}

    def to_core(q):
        for k in FAR + (0,):

            def pick(z, carry):
                for h, (dense, _, _) in enumerate(HALVES):
                    there = (net.on(dense) + k) % NRING
                    core_out[h][q, k, z] = total(h, q, (1 - net.c) * 32 + there * NZ + z).astype(BF)
                return carry

            lax.fori_loop(0, NZ, pick, 0, unroll=NZ)
        for h in range(2):
            cores[q, h] = Channel(net, core_in[h].at[q])
            cores[q, h].copy(core_out[h].at[q], core_in[h].at[q], "c", 1)

    def to_ring(q):
        for h in range(2):
            cores[q, h].wait_recv()
            mids[q, h] = Channel(net, ring_in[h].at[q, pl.ds(0, 3)])
        for k in FAR + (0,):

            def join(z, carry):
                for h, (dense, _, _) in enumerate(HALVES):
                    there = (net.on(dense) + k) % NRING
                    both = total(h, q, net.c * 32 + there * NZ + z) + core_in[h][q, k, z].astype(F32)
                    if k:
                        ring_out[h][q, k, z] = both.astype(BF)
                    else:
                        ring_own[h][q, z] = both
                return carry

            lax.fori_loop(0, NZ, join, 0, unroll=NZ)
            if k:
                for h, (dense, _, _) in enumerate(HALVES):
                    mids[q, h].copy(ring_out[h].at[q, k], ring_in[h].at[q, k], dense, k)

    accumulate(0, tuple(range(NQ)))
    for q in range(NQ):
        accumulate(1, (q,))
        to_core(q)
        if q:
            to_ring(q - 1)
    to_ring(NQ - 1)
    zc = {}
    for q in range(NQ):
        for h in range(2):
            mids[q, h].wait_recv()

        def ring(z, carry):
            for h in range(2):
                both = ring_own[h][q, z]
                for k in NEAR:
                    both = both + ring_in[h][q, k, z].astype(F32)
                zout[q, z, h * CH:(h + 1) * CH] = both.astype(BF)
                zown[q, z, h * CH:(h + 1) * CH] = both
            return carry

        lax.fori_loop(0, NZ, ring, 0, unroll=NZ)
        zc[q] = Channel(net, zin.at[q, pl.ds(0, NZ - 1)])
        for k in ZFAR:
            zc[q].copy(zout.at[q, (net.z + k) % NZ], zin.at[q, k], "z", k)
    for q in range(NQ):
        grad = zown[q, net.z]
        zc[q].wait_recv()
        for k in ZNEAR:
            grad = grad + zin[q, k].astype(F32)
        est[q] = jnp.maximum(est[q] - STEP * grad, 0.0)
        done(q)


def kernel(owner, inner_id, res, psf, mask, sky, observed, resample, psf_mats, out,
           idtile, seen, tab, tabs, r32, p32, rm, rt, pm, pt, obs, est, held, local, send, recv,
           gz, *rest):
    full = (rest[:NQ], rest[NQ:2 * NQ])
    (slots_a, slots_b, got_a0, got_a1, got_b0, got_b1, back, rows_a, rows_b, cum_a, cum_b,
     co_a, co_b, ci_a, ci_b, ro_a, ro_b, rw_a, rw_b, ri_a, ri_b, zout, zown, zin) = rest[2 * NQ:]
    got = ((got_a0, got_a1), (got_b0, got_b1))
    slots, rows = (slots_a, slots_b), (rows_a, rows_b)
    cum, core_out, core_in = (cum_a, cum_b), (co_a, co_b), (ci_a, ci_b)
    ring_out, ring_own, ring_in = (ro_a, ro_b), (rw_a, rw_b), (ri_a, ri_b)
    net = Net(send, recv)

    def fetch(src, dst, i):
        cp = pltpu.make_async_copy(src, dst, local.at[i])
        cp.start()
        return cp

    starts = [fetch(sky.at[net.own, pl.ds(h * HALF + q * CH, CH)], est.at[q, pl.ds(h * CH, CH)], h * NQ + q)
              for q in range(NQ) for h in range(2)]
    mats = [fetch(resample, r32, 8), fetch(psf_mats, p32, 9)]
    blocks = fetch(observed, obs, 10)
    own_ids = [owner[0, r] * 8 + inner_id[0, r] for r in range(REQ)]
    idtile[...] = id_tile(own_ids)
    net.barrier()
    told = []
    for h, (_, sparse, _) in enumerate(HALVES):
        told.append(Channel(net, seen.at[h, pl.ds(0, 3)]))
        for k in NEAR:
            told[h].copy(idtile, seen.at[h, k], sparse, k)
        seen[h, 0] = idtile[...]
    for cp in starts:
        cp.wait()
    zc = {q: send_block(net, est, gz, q) for q in range(NQ)}
    for cp in told:
        cp.wait_recv()
    tables(net, seen, tab)
    to_scalar = fetch(tab, tabs, 11)
    for cp in mats:
        cp.wait()

    def cast(i, carry):
        rm[i] = r32[i].astype(BF)
        rt[i] = r32[i].T.astype(BF)
        pm[i] = p32[i].astype(BF)
        pt[i] = p32[i].T.astype(BF)
        return carry

    lax.fori_loop(0, 16, cast, 0, unroll=2)
    to_scalar.wait()
    first = net.used
    for iteration in range(ITERS):
        last = gather(net, zc, gz, full, slots, got, tabs)
        if iteration == 0:
            blocks.wait()
        gathering, net.open = net.open, []
        copies = {}
        for group in range(2):
            for cp in last[group]:
                cp.wait_recv()
            products(group, got, back, owner, inner_id, res, psf, obs, mask, rm, rt, pm, pt)
            if group:
                wait_sends(gathering)
            copies[group] = send_rows(net, group, back, rows)
        zc, ring, cores = {}, [], []

        def done(q):
            if iteration < ITERS - 1:
                zc[q] = send_block(net, est, gz, q)
                return
            held[q, net.own] = est[q]
            mine = held.at[q, net.own]
            cores.append(Channel(net, mine))
            cores[-1].copy(mine, mine, "c", 1)
            for k in FAR:
                ring.append((q, k, Channel(net, mine)))
                ring[-1][2].copy(mine, mine, "y", k)

        scatter(net, copies, back, rows, cum, core_out, core_in, ring_out, ring_own, ring_in,
                zout, zown, zin, est, tabs, done)
        if iteration < ITERS - 1:
            ahead = [zc[q] for q in range(NQ)]
            wait_sends([cp for cp in net.open if not any(cp is other for other in ahead)])
            net.open = ahead
            net.used = first
    for q, k, cp in ring:
        cp.wait_recv()
        there = held.at[q, ((net.y - k + NRING) % NRING) * 2 + net.c]
        cores.append(Channel(net, there))
        cores[-1].copy(there, there, "c", 1)
    for cp in cores:
        cp.wait_recv()
    for q in range(NQ):
        for h in range(2):
            out[:, h * HALF + q * CH:h * HALF + (q + 1) * CH] = held[q, :, h * CH:(h + 1) * CH]
    wait_sends(net.open)


def twice(*shape_dtype):
    return [pltpu.VMEM(*shape_dtype)] * 2


SCRATCH = (
    [pltpu.VMEM((8, B), I32), pltpu.VMEM((2, NRING, 8, B), I32), pltpu.VMEM((8, B), I32), pltpu.SMEM((8, B), I32)]
    + twice((16, B, B), F32) + twice((16, B, B), BF) + twice((16, B, B), BF)
    + [pltpu.VMEM((REQ, EXPO, B, B), BF), pltpu.VMEM((NQ, 2 * CH, B), F32), pltpu.VMEM((NQ, 8, 2 * CH, B), F32)]
    + [pltpu.SemaphoreType.DMA((12,)), pltpu.SemaphoreType.DMA((SEMS,)), pltpu.SemaphoreType.DMA((SEMS,))]
    + [pltpu.VMEM((NQ, NZ, 2 * CH, B), BF)]
    + [pltpu.VMEM((64, CH, B), BF)] * (2 * NQ) + twice((NRING, NQ, REQ, CH, B), BF)
    + twice((NRING, NQ, GROUP, CH, B), BF) + twice((NRING, NQ, GROUP, CH, B), BF)
    + [pltpu.VMEM((REQ, B, B), BF)]
    + twice((NRING, REQ, HALF, B), BF) + twice((NQ, 64, CH, B), F32)
    + twice((NQ, NRING, NZ, CH, B), BF) + twice((NQ, NRING, NZ, CH, B), BF)
    + twice((NQ, NRING, NZ, CH, B), BF) + twice((NQ, NZ, CH, B), F32) + twice((NQ, NRING, NZ, CH, B), BF)
    + [pltpu.VMEM((NQ, NZ, 2 * CH, B), BF), pltpu.VMEM((NQ, NZ, 2 * CH, B), F32), pltpu.VMEM((NQ, NZ, 2 * CH, B), BF)]
)


def on_device(sky, observed, src_owner, src_local, res_ids, psf_ids, pixel_mask, resample, psf):
    vm = pl.BlockSpec(memory_space=pltpu.VMEM)
    sm = pl.BlockSpec(memory_space=pltpu.SMEM)
    hbm = pl.BlockSpec(memory_space=pl.ANY)
    return pl.pallas_call(
        kernel, name="landweber",
        out_shape=jax.ShapeDtypeStruct((8, B, B), F32),
        in_specs=[sm, sm, sm, sm, vm, hbm, hbm, hbm, hbm], out_specs=vm,
        scratch_shapes=SCRATCH,
        compiler_params=pltpu.CompilerParams(
            collective_id=0, has_side_effects=True, vmem_limit_bytes=60 * 2**20),
    )(src_owner, src_local, jnp.swapaxes(res_ids, 1, 2)[0], jnp.swapaxes(psf_ids, 1, 2)[0], pixel_mask[0],
      sky, observed[0], resample, psf)


def solution(mesh):
    in_specs = (
        P("sky", None, None),
        P("exp", "sky", None, None, None),
        P("exp", "sky"),
        P("exp", "sky"),
        P("exp", "sky", None),
        P("exp", "sky", None),
        P("exp", "sky", None, None, None),
        P(),
        P(),
    )
    return jax.shard_map(
        on_device, mesh=mesh, in_specs=in_specs, out_specs=P("sky", None, None), check_vma=False
    )
```

time: 126 us -> 117 us (0.929)
  Pallas kernels: 123 us -> 115 us
    pallas_call x1, Pallas kernels: 123 us -> 115 us  [on_device(): pl.pallas_call(kernel, name='landweber', out_shape=jax.ShapeDtypeStruct((...]
where the time goes in v3:
time: 117 us
  Pallas kernels  115 us (98%)
  local copies, waits for them, and re-layouts  1.87 us (2%)
    pallas_call x1, Pallas kernels, on_device(): pl.pallas_call(kernel, name='landweber', out_shape=jax.ShapeDtypeStruct((...  115 us

profile of v3, /device:TPU:1, one launch (start us, length us, event | category | flops | bytes accessed | tf_op | source)
XLA Modules:
  0.0 117.1 jit_solution(7062111937001970105)
XLA Ops:
  0.0 115.3 %landweber.1 = f32[8,128,128]{2,1,0:T(8,128)} custom-call(s32[1,16]{1,0:T(1,128)} %owner.1, s32[1,16]{1,0:T(1,128)} %inner_id.1, s32[4,16]{1,0:T(4,128)} %bitcast.10, s32[4,16]{1,0:T(4,128)} %bitcast.11, s32[16,4,2,128]{3,2,1,0:T(2,128)} %bitcast.9, f32[8,128,128]{2,1,0:T(8,128)} %sky.1, bf16[16,4,128,128]{3,2,1,0:T(8,128)(2,1)} %bitcast.8, ...), custom_call_target="tpu_custom_call" | custom-call | tf_op jit(solution)/shard_map/landweber/pallas_call | solution.py:437
  115.3 1.9 %copy.11 = f32[8,128,128]{2,1,0:T(8,128)} copy(f32[8,128,128]{2,1,0:T(8,128)} %landweber.1) | data formatting | bytes 1048576

commit v4 on v3

--- a/solution.py
+++ b/solution.py
@@ -194,11 +194,11 @@
                           preferred_element_type=F32).astype(BF)
 
     def two(i, carry):
-        for j in range(4):
-            row(4 * i + j)
+        for j in range(GROUP):
+            row(j)
         return carry
 
-    lax.fori_loop(0, GROUP // 4, two, 0)
+    lax.fori_loop(0, 1, two, 0)
 
 
 def send_rows(net, group, back, rows):

time: 117 us -> 117 us (level)
  no operation moved by 1% of the time
where the time goes in v4:
time: 117 us
  Pallas kernels  115 us (98%)
  local copies, waits for them, and re-layouts  1.87 us (2%)
    pallas_call x1, Pallas kernels, on_device(): pl.pallas_call(kernel, name='landweber', out_shape=jax.ShapeDtypeStruct((...  115 us

profile of v4, /device:TPU:1, one launch (start us, length us, event | category | flops | bytes accessed | tf_op | source)
XLA Modules:
  0.0 116.5 jit_solution(382486907457494266)
XLA Ops:
  0.0 114.7 %landweber.1 = f32[8,128,128]{2,1,0:T(8,128)} custom-call(s32[1,16]{1,0:T(1,128)} %owner.1, s32[1,16]{1,0:T(1,128)} %inner_id.1, s32[4,16]{1,0:T(4,128)} %bitcast.10, s32[4,16]{1,0:T(4,128)} %bitcast.11, s32[16,4,2,128]{3,2,1,0:T(2,128)} %bitcast.9, f32[8,128,128]{2,1,0:T(8,128)} %sky.1, bf16[16,4,128,128]{3,2,1,0:T(8,128)(2,1)} %bitcast.8, ...), custom_call_target="tpu_custom_call" | custom-call | tf_op jit(solution)/shard_map/landweber/pallas_call | solution.py:437
  114.7 1.9 %copy.11 = f32[8,128,128]{2,1,0:T(8,128)} copy(f32[8,128,128]{2,1,0:T(8,128)} %landweber.1) | data formatting | bytes 1048576
